TPU v7x, 256 devices: a whole 4x4x8 slice. The times are simulated.
256 devices in a mesh: tier: 8 (over z), aux: 32 (over y, x, core).
Axes of the slice: x: 4, y: 4, z: 8, core: 2. Of those that a mesh axis runs over, the one named last changes fastest.
Arguments:
- section_state: float32 [2048, 18432], P(('tier', 'aux')), may hold values from -6 to 6
- coupling: float32 [96, 96], replicated, may hold values from -0.625 to 0.625
- site_energy: float32 [96], replicated, may hold values from -1 to 1
- bath_rate: float32 [96], replicated, may hold values from 0.3 to 3
- bath_strength: float32 [96], replicated, may hold values from 0.1 to 1
- bath_of_site: int32 [96], replicated, may hold values from 0 to 95, each once
- quanta: int32 [2048, 4], P(('tier', 'aux')), may hold values from -1 to 95, as said below
- send_list: int32 [256, 128], P(('tier', 'aux')), may hold values from -1 to 31, as said below
- dest_slot: int32 [256, 128], P(('tier', 'aux')), may hold values from 0 to 7
Outputs:
- derivative: float32 [2048, 18432], P(('tier', 'aux'))
Inputs may be any that keep to these rules, and one draw needn't show every extreme that they name: Row a lists the sites of auxiliary a's quanta, 1 to 4 of them with repeats allowed, in ascending order, then -1 in the empty places. `send_list`: entry [d, l] is slot * 4 + place for an auxiliary slot of device d, or -1. The first place of every distinct site of every auxiliary stands in exactly one lane of its device, and no other place stands anywhere. On every device the 2 lanes of group 0 towards one aux index are all used.
All inputs are finite; a program needn't handle non-finite values.
Results may differ from a plain program's by a relative error of at most 0.00005.
Values sent between devices are 32-bit elements; how exact they have to be, the bound alone decides.
A program may use at most 64 MiB of HBM per device.

v0:
```python
import jax
import jax.numpy as jnp
from jax import lax
from jax.sharding import PartitionSpec as P

thermal = 0.5
highest = lax.Precision.HIGHEST


def passed_along(value, axis, steps):
    count = lax.axis_size(axis)
    first, last = (max(0, -steps), min(count, count - steps))
    return lax.ppermute(value, axis, [(source, source + steps) for source in range(first, last)])


def take_slices(states, holders, columns):
    site_count = states.shape[1]
    flat_holders = holders.reshape(-1)
    flat_columns = columns.reshape(-1)
    positions = jnp.arange(site_count, dtype=jnp.int32)
    row_part = states[flat_holders, flat_columns, :]
    column_real = states[flat_holders[:, None], positions[None, :], flat_columns[:, None]]
    column_imag = states[
        flat_holders[:, None], positions[None, :], flat_columns[:, None] + site_count
    ]
    joined = jnp.concatenate([row_part, column_real, column_imag], axis=-1)
    return joined.reshape(holders.shape + (4 * site_count,))


def descend(payload_pair):
    return passed_along(payload_pair, "tier", -1)


def ascend(reply_block):
    return passed_along(reply_block, "tier", 1)


def answer(states, labels):
    slot_ids = labels[..., 0]
    wanted = labels[..., 1]
    picked = take_slices(states, slot_ids, jnp.maximum(wanted, 0))
    return jnp.where((wanted >= 0)[..., None], picked, 0.0)


def trade_edges(states, payload, labels):
    inbound = lax.all_to_all(payload, "aux", split_axis=1, concat_axis=1, tiled=True)
    inbound_tags = lax.all_to_all(labels, "aux", split_axis=1, concat_axis=1, tiled=True)
    lower_in, lower_tags = descend((inbound[1], inbound_tags[1]))
    lower_reply = ascend(answer(states, lower_tags))
    replies = jnp.stack([answer(states, inbound_tags[0]), lower_reply])
    arrived = jnp.stack([inbound[0], lower_in])
    arrived_tags = jnp.stack([inbound_tags[0], lower_tags])
    returned = lax.all_to_all(replies, "aux", split_axis=1, concat_axis=1, tiled=True)
    return (returned, arrived, arrived_tags)


def on_device(
    section_state,
    coupling,
    site_energy,
    bath_rate,
    bath_strength,
    bath_of_site,
    quanta,
    send_list,
    dest_slot,
):
    site_count = coupling.shape[0]
    doubled_width = 2 * site_count
    aux_count = section_state.shape[0]
    flat_shape = section_state.shape
    section_state = section_state.reshape(aux_count, site_count, doubled_width)
    depth_count = quanta.shape[1]
    lane_count = send_list.shape[1]
    peer_count = lax.axis_size("aux")
    capacity = lane_count // (2 * peer_count)
    band_index = lax.axis_index("tier")
    positions = jnp.arange(site_count, dtype=jnp.int32)
    hamilton = (coupling + coupling.T) * 0.5 + jnp.diag(site_energy)
    zero_block = jnp.zeros_like(hamilton)
    paired = jnp.concatenate(
        [jnp.concatenate([hamilton, zero_block], 1), jnp.concatenate([zero_block, hamilton], 1)], 0
    )
    chooser = (bath_of_site[:, None] == positions[None, :]).astype(jnp.float32)
    site_params = jnp.dot(chooser, jnp.stack([bath_rate, bath_strength], axis=1), precision=highest)
    site_rate = site_params[:, 0]
    site_strength = site_params[:, 1]
    real_coef = 2.0 * thermal * site_strength
    imag_coef = site_strength * site_rate
    matches = (quanta[:, :, None] == positions[None, None, :]).astype(jnp.float32)
    multiple = jnp.sum(matches, axis=1)
    damping = jnp.dot(multiple, site_rate, precision=highest)
    entries = send_list[0]
    clipped = jnp.maximum(entries, 0)
    sources = clipped // depth_count
    lane_sites = quanta[sources, clipped % depth_count]
    lane_ids = jnp.arange(lane_count, dtype=jnp.int32)
    lane_group = lane_ids // (peer_count * capacity)
    usable = (entries >= 0) & (lane_sites >= 0) & (band_index - lane_group >= 0)
    lane_columns = jnp.maximum(lane_sites, 0)
    outgoing = jnp.where(usable[:, None], take_slices(section_state, sources, lane_columns), 0.0)
    labels = jnp.stack([dest_slot[0], jnp.where(usable, lane_sites, -1)], axis=-1)
    outgoing = outgoing.reshape(2, peer_count, capacity, 4 * site_count)
    labels = labels.reshape(2, peer_count, capacity, 2)
    returned, arrived, arrived_tags = trade_edges(section_state, outgoing, labels)
    left_product = jnp.einsum("ij,ajc->aic", hamilton, section_state, precision=highest)
    right_product = jnp.dot(
        section_state.reshape(-1, doubled_width), paired, precision=highest
    ).reshape(section_state.shape)
    commutator = left_product - right_product
    coherent = jnp.concatenate(
        [commutator[..., site_count:], -commutator[..., :site_count]], axis=-1
    )
    local_part = coherent - damping[:, None, None] * section_state
    arrived = arrived.reshape(-1, 4 * site_count)
    arrived_tags = arrived_tags.reshape(-1, 2)
    up_sites = arrived_tags[:, 1]
    up_usable = up_sites >= 0
    up_slot = jnp.where(up_usable, arrived_tags[:, 0], 0)
    up_site = jnp.maximum(up_sites, 0)
    up_data = jnp.concatenate(
        [
            arrived[:, site_count : 2 * site_count],
            -arrived[:, :site_count],
            -arrived[:, 3 * site_count :],
            arrived[:, 2 * site_count : 3 * site_count],
        ],
        axis=-1,
    )
    up_data = jnp.where(up_usable[:, None], up_data, 0.0)
    returned = returned.reshape(lane_count, 4 * site_count)
    lane_onehot = (lane_columns[:, None] == positions[None, :]).astype(jnp.float32)
    weights = jnp.sum(lane_onehot * multiple[sources], axis=1)
    lane_coefs = jnp.dot(lane_onehot, jnp.stack([real_coef, imag_coef], axis=1), precision=highest)
    shared = (-weights * lane_coefs[:, 1])[:, None]
    row_turn = (-weights * lane_coefs[:, 0])[:, None]
    column_turn = (weights * lane_coefs[:, 0])[:, None]
    row_real = returned[:, :site_count]
    row_imag = returned[:, site_count : 2 * site_count]
    column_real = returned[:, 2 * site_count : 3 * site_count]
    column_imag = returned[:, 3 * site_count :]
    down_data = jnp.concatenate(
        [
            shared * row_real - row_turn * row_imag,
            shared * row_imag + row_turn * row_real,
            shared * column_real - column_turn * column_imag,
            shared * column_imag + column_turn * column_real,
        ],
        axis=-1,
    )
    down_data = jnp.where(usable[:, None], down_data, 0.0)
    all_data = jnp.concatenate([up_data, down_data], axis=0)
    all_slot = jnp.concatenate([up_slot, sources], axis=0).astype(jnp.int32)
    all_site = jnp.concatenate([up_site, lane_columns], axis=0).astype(jnp.int32)
    result = local_part.at[all_slot, all_site, :].add(all_data[:, :doubled_width])
    result = result.at[all_slot[:, None], positions[None, :], all_site[:, None]].add(
        all_data[:, doubled_width : doubled_width + site_count]
    )
    result = result.at[all_slot[:, None], positions[None, :], all_site[:, None] + site_count].add(
        all_data[:, doubled_width + site_count :]
    )
    return result.reshape(flat_shape)


def solution(mesh):
    return jax.shard_map(
        on_device,
        mesh=mesh,
        in_specs=(
            P(("tier", "aux"), None),
            P(),
            P(),
            P(),
            P(),
            P(),
            P(("tier", "aux"), None),
            P(("tier", "aux"), None),
            P(("tier", "aux"), None),
        ),
        out_specs=P(("tier", "aux"), None),
        check_vma=False,
    )
```

profile of v0, /device:TPU:128, one launch (start us, length us, event | category | flops | bytes accessed | tf_op | source)
XLA Modules:
  0.0 871.9 jit_solution(12243883787793019891)
XLA Ops:
  0.0 0.7 fusion.80
  0.7 0.7 compare_bitcast_fusion.3
  1.4 1.8 gather_fusion
  3.5 0.5 broadcast.1243
  4.1 1.3 reduce.17
  5.6 0.7 copy.136
  6.3 7.3 all-to-all-start
  13.6 0.3 reshape_reshape.3
  14.0 0.3 reshape.735
  14.3 0.3 copy-done
  15.0 1.3 convolution_bitcast_fusion.1
  16.3 0.3 copy.135
  16.6 0.8 fusion
  17.4 0.2 fusion.89
  17.6 0.5 copy-done.7
  18.1 0.2 fusion.27
  18.2 0.2 convolution_bitcast_fusion.2
  18.7 120.8 %gather_fusion.3 = f32[12288]{0:T(1024)S(1)} fusion(f32[8,96,192]{2,1,0:T(8,128)S(1)} %reshape.735, s32[12288]{0:T(1024)S(1)} %reshape.771), kind=kCustom, calls=%fused_computation.3 | custom fusion | bytes 245760 | tf_op jit(solution)/shard_map/gather | solution.py:23
  139.7 120.8 %gather_fusion.2 = f32[12288]{0:T(1024)S(1)} fusion(f32[8,96,192]{2,1,0:T(8,128)S(1)} %reshape.735, s32[12288]{0:T(1024)S(1)} %reshape.765), kind=kCustom, calls=%fused_computation.2 | custom fusion | bytes 245760 | tf_op jit(solution)/shard_map/gather | solution.py:22
  260.6 1.3 gather_fusion.1
  262.1 0.2 ge.87
  262.3 0.6 gather_fusion.4
  263.0 0.2 select_reduce_fusion
  263.2 0.2 fusion.21
  263.4 0.4 maximum_subtract_fusion
  263.8 0.3 maximum_select_fusion
  264.1 0.7 copy.142
  264.9 7.4 all-to-all-start.1
  272.8 2.2 collective-permute-start
  275.8 60.7 %gather_fusion.7 = f32[6144]{0:T(1024)S(1)} fusion(f32[8,96,192]{2,1,0:T(8,128)S(1)} %reshape.735, s32[6144]{0:T(1024)S(1)} %reshape.797), kind=kCustom, calls=%fused_computation.7 | custom fusion | bytes 122880 | tf_op jit(solution)/shard_map/gather | solution.py:23
  336.6 60.7 %gather_fusion.6 = f32[6144]{0:T(1024)S(1)} fusion(f32[8,96,192]{2,1,0:T(8,128)S(1)} %reshape.735, s32[6144]{0:T(1024)S(1)} %reshape.791), kind=kCustom, calls=%fused_computation.6 | custom fusion | bytes 122880 | tf_op jit(solution)/shard_map/gather | solution.py:22
  397.6 0.9 gather_fusion.5
  400.3 60.7 %gather_fusion.10 = f32[6144]{0:T(1024)S(1)} fusion(f32[8,96,192]{2,1,0:T(8,128)S(1)} %reshape.735, s32[6144]{0:T(1024)S(1)} %reshape.815), kind=kCustom, calls=%fused_computation.10 | custom fusion | bytes 122880 | tf_op jit(solution)/shard_map/gather | solution.py:23
  461.1 60.7 %gather_fusion.9 = f32[6144]{0:T(1024)S(1)} fusion(f32[8,96,192]{2,1,0:T(8,128)S(1)} %reshape.735, s32[6144]{0:T(1024)S(1)} %reshape.809), kind=kCustom, calls=%fused_computation.9 | custom fusion | bytes 122880 | tf_op jit(solution)/shard_map/gather | solution.py:22
  522.1 0.9 gather_fusion.8
  523.4 3.8 collective-permute-start.2
  528.2 3.2 collective-permute-start.1
  531.4 0.8 pad_maximum_fusion.1
  532.2 7.4 all-to-all-start.2
  540.0 0.2 maximum_select_fusion.1
  540.1 7.7 all-to-all-done.2
  548.0 0.2 multiply_subtract_fusion.1
  548.2 0.2 maximum_select_fusion.2
  548.5 13.6 %scatter_fusion = f32[8,96,192]{2,1,0:T(8,128)S(1)} fusion(f32[8,96,192]{2,1,0:T(8,128)S(1)} %maximum_subtract_fusion, s32[256]{0:T(256)S(1)} %bitcast.148, f32[256,192]{1,0:T(8,128)S(1)} %fusion.14), kind=kCustom, calls=%fused_computation.11 | custom fusion | flops 49152 | bytes 591872 | tf_op jit(solution)/shard_map/scatter-add | solution.py:155
  562.1 0.4 reshape.744
  562.8 154.1 %scatter_fusion.1 = f32[147456]{0:T(1024)S(1)} fusion(f32[147456]{0:T(1024)S(1)} %reshape.744, s32[24576]{0:T(1024)S(1)} %reshape.827, f32[24576]{0:T(1024)S(1)} %reshape.829), kind=kCustom, calls=%fused_computation.12 | custom fusion | flops 24576 | bytes 393216
  716.9 154.1 %scatter_fusion.2 = f32[147456]{0:T(1024)S(1)} fusion(f32[147456]{0:T(1024)S(1)} %scatter_fusion.1, s32[24576]{0:T(1024)S(1)} %reshape.833, f32[24576]{0:T(1024)S(1)} %reshape.835), kind=kCustom, calls=%fused_computation.13 | custom fusion | flops 24576 | bytes 393216
  871.0 0.9 reshape.742
  (128 shorter events, 7.6 us)
Async XLA Ops:
  0.0 13.6 %copy-start.1 = (f32[8,18432]{1,0:T(8,128)S(1)}, f32[8,18432]{1,0:T(8,128)}, u32[]{:S(2)}) copy-start(f32[8,18432]{1,0:T(8,128)} %param.9) | copy-start | bytes 1769476
  6.3 258.6 %all-to-all-start = ((s32[2,32,2,2]{2,0,3,1:T(2,128)}), s32[2,32,2,2]{2,0,3,1:T(2,128)S(1)}, u32[]{:S(2)}, u32[]{:S(2)}) async-start(s32[2,32,2,2]{2,0,3,1:T(2,128)} %copy.136), calls=%async_computation | async-start | bytes 131072 | tf_op jit(solution)/shard_map/all_to_all | solution.py:47
  13.9 0.7 copy-start
  14.0 0.8 copy-start.3
  14.0 0.8 copy-start.2
  14.0 0.9 copy-start.4
  17.4 0.7 copy-start.7
  17.4 0.7 copy-start.8
  17.4 0.7 copy-start.9
  264.9 263.3 %all-to-all-start.1 = ((f32[2,32,2,384]{3,2,0,1:T(2,128)}), f32[2,32,2,384]{3,2,0,1:T(2,128)S(1)}, u32[]{:S(2)}, u32[]{:S(2)}) async-start(f32[2,32,2,384]{3,2,0,1:T(2,128)} %copy.142), calls=%async_computation.1 | async-start | bytes 393216 | tf_op jit(solution)/shard_map/all_to_all | solution.py:46
  272.8 126.0 %collective-permute-start = (s32[32,2,2]{0,1,2:T(2,128)S(1)}, s32[32,2,2]{0,1,2:T(2,128)S(1)}, u32[]{:S(2)}, u32[]{:S(2)}) collective-permute-start(s32[32,2,2]{0,1,2:T(2,128)S(1)} %copy.139), channel_id=1, source_target_pairs={{32,0},{64,32},{96,64},{128,96},{160,128},{192,160},{224,192},{33,... | collective-permute-start | bytes 1544 | tf_op jit(solution)/shard_map/ppermute | solution.py:13
  522.1 5.3 copy-start.6
  523.0 4.5 copy-start.5
  523.4 8.0 collective-permute-start.2
  528.2 11.4 %collective-permute-start.1 = (f32[32,2,384]{2,1,0:T(2,128)S(1)}, f32[32,2,384]{2,1,0:T(2,128)S(1)}, u32[]{:S(2)}, u32[]{:S(2)}) collective-permute-start(f32[32,2,384]{2,1,0:T(2,128)S(1)} %get-tuple-element.28), channel_id=1, source_target_pairs={{32,0},{64,32},{96,64},{128,96},{160,128},{192,160},{224,192},{33,... | collective-permute-start | bytes 294920 | tf_op jit(solution)/shard_map/ppermute | solution.py:13
  532.2 15.6 %all-to-all-start.2 = ((f32[2,32,2,384]{3,2,0,1:T(2,128)}), f32[2,32,2,384]{3,2,0,1:T(2,128)S(1)}, u32[]{:S(2)}, u32[]{:S(2)}) async-start(f32[2,32,2,384]{3,2,0,1:T(2,128)} %pad_maximum_fusion.1), calls=%async_computation.2 | async-start | bytes 393216 | tf_op jit(solution)/shard_map/all_to_all | solution.py:53
where the time goes:
time: 873 us; the launch traced here: 872 us
  local copies, waits for them, and re-layouts  501 us (57%)
  other arithmetic  329 us (38%)
  starting transfers between devices  31.3 us (4%)
    unnamed x7, other arithmetic  310 us
    gather x5, local copies, waits for them, and re-layouts, take_slices(): states[flat_holders[:, None], positions[None, :], flat_columns[:, None] +...  242 us
    gather x5, local copies, waits for them, and re-layouts, take_slices(): states[flat_holders[:, None], positions[None, :], flat_columns[:, None]]  242 us
  transfers between devices with their start and end apart: 6, of which 1 were waited for; matrix products, arithmetic and copies ran while one was open for 57% of the time, Pallas kernels for 0%

commit v1 on v0

v1 whole, which is shorter than its diff:
```python
import functools

import jax
import jax.numpy as jnp
from jax import lax
from jax.experimental import pallas as pl
from jax.experimental.pallas import tpu as pltpu
from jax.sharding import PartitionSpec as P

MESH = pl.DeviceIdType.MESH
F32 = jnp.float32
BF16 = jnp.bfloat16
SITES = 96
HALF = 48
SLOTS = 8
DEPTH = 4
PEERS = 32
TILES = 2 * PEERS
LANES = 128
TIERS = 8


def split_pair(value):
    high = value.astype(BF16)
    return high, (value - high.astype(F32)).astype(BF16)


def mxu(left, right):
    return jnp.dot(left, right, preferred_element_type=F32)


def permuted(site):
    return (site >> 1) + HALF * (site & 1)


def kernel(
    state_hbm,
    coupling_hbm,
    energy_hbm,
    rate_hbm,
    strength_hbm,
    bath_hbm,
    quanta_hbm,
    send_hbm,
    dest_hbm,
    result,
    raw,
    coupling_v,
    table_v,
    bath_v,
    quanta_v,
    send_v,
    dest_v,
    tag_out,
    tag_in,
    up_out,
    up_in,
    reply_out,
    reply_in,
    tag_cols,
    own_cols,
    rows_hi,
    rows_lo,
    cols_hi,
    cols_lo,
    total,
    load_sem,
    small_sem,
    send_sem,
    recv_sem,
):
    tier = lax.axis_index("tier")
    peer = lax.axis_index("aux")
    my_y = peer // 8
    my_x = lax.rem(peer, 8) // 2
    my_c = lax.rem(peer, 2)

    def far_first(step):
        def offset(k):
            return jnp.where(k == 0, 2, jnp.where(k == 1, 1, jnp.where(k == 2, 3, 0)))

        dy = offset(step // 8)
        dx = offset(lax.rem(step, 8) // 2)
        dc = 1 - lax.rem(step, 2)
        return lax.rem(my_y + dy, 4) * 8 + lax.rem(my_x + dx, 4) * 2 + lax.rem(my_c + dc, 2)

    barrier = pltpu.get_barrier_semaphore()

    @pl.when(tier < TIERS - 1)
    def _():
        def greet_above(step, carry):
            pl.semaphore_signal(
                barrier, inc=1, device_id=(tier + 1, far_first(step)), device_id_type=MESH
            )
            return carry

        lax.fori_loop(0, PEERS, greet_above, 0)

    def greet_band(step, carry):
        pl.semaphore_signal(
            barrier, inc=1, device_id=(tier, far_first(step)), device_id_type=MESH
        )
        return carry

    lax.fori_loop(0, PEERS - 1, greet_band, 0)

    small = [
        pltpu.make_async_copy(send_hbm, send_v, small_sem.at[0]),
        pltpu.make_async_copy(dest_hbm, dest_v, small_sem.at[1]),
        pltpu.make_async_copy(quanta_hbm, quanta_v, small_sem.at[2]),
        pltpu.make_async_copy(rate_hbm, table_v.at[0], small_sem.at[3]),
        pltpu.make_async_copy(strength_hbm, table_v.at[1], small_sem.at[4]),
        pltpu.make_async_copy(energy_hbm, table_v.at[2], small_sem.at[5]),
        pltpu.make_async_copy(bath_hbm, bath_v, small_sem.at[6]),
        pltpu.make_async_copy(coupling_hbm, coupling_v, small_sem.at[7]),
    ]
    for copy in small:
        copy.start()
    load = pltpu.make_async_copy(state_hbm, raw, load_sem)
    load.start()
    for copy in small:
        copy.wait()

    lane = lax.broadcasted_iota(jnp.int32, (1, LANES), 1)
    sub8 = lax.broadcasted_iota(jnp.int32, (SLOTS, LANES), 0)
    sub96 = lax.broadcasted_iota(jnp.int32, (SITES, LANES), 0)
    quanta = jnp.concatenate(
        [
            jnp.concatenate([quanta_v[...], jnp.zeros((DEPTH, LANES - SLOTS), jnp.int32)], axis=1),
            jnp.zeros((SLOTS - DEPTH, LANES), jnp.int32),
        ],
        axis=0,
    ).T[:SLOTS]

    def quanta_of(entry):
        slot = entry >> 2
        place = entry & 3
        hit = sub8 == jnp.broadcast_to(slot, (SLOTS, LANES))
        found = [
            jnp.sum(
                jnp.where(hit, jnp.broadcast_to(quanta[:, p : p + 1], (SLOTS, LANES)), 0),
                axis=0,
                keepdims=True,
            )
            for p in range(DEPTH)
        ]
        site = found[3]
        for p in range(DEPTH - 1):
            site = jnp.where(place == p, found[p], site)
        count = sum((found[p] == site).astype(F32) for p in range(DEPTH))
        return slot, site, count

    pad = jnp.zeros((1, LANES - SITES), F32)
    base = jnp.concatenate(
        [
            jnp.concatenate([bath_v[...].astype(F32), pad], axis=1),
            jnp.concatenate([table_v[0], pad], axis=1),
            jnp.concatenate([table_v[1], pad], axis=1),
            jnp.concatenate([table_v[2], pad], axis=1),
            jnp.zeros((LANES - 4, LANES), F32),
        ],
        axis=0,
    ).T
    bath_col = base[:SITES, 0:1]
    rate_col = base[:SITES, 1:2]
    strength_col = base[:SITES, 2:3]
    sub96f = sub96.astype(F32)

    def look_up(site, columns):
        hit = sub96 == jnp.broadcast_to(site, (SITES, LANES))
        bath = jnp.sum(
            jnp.where(hit, jnp.broadcast_to(bath_col, (SITES, LANES)), 0.0), axis=0, keepdims=True
        )
        hit = sub96f == jnp.broadcast_to(bath, (SITES, LANES))
        return [
            jnp.sum(
                jnp.where(hit, jnp.broadcast_to(column, (SITES, LANES)), 0.0), axis=0, keepdims=True
            )
            for column in columns
        ]

    entry = send_v[...]
    slot, site, weight = quanta_of(jnp.maximum(entry, 0))
    group = lane // (LANES // 2)
    usable = (entry >= 0) & (site >= 0) & (tier - group >= 0)
    strength_l, rate_l = look_up(site, [strength_col, rate_col])
    lower = dest_v[...]

    def marked(value):
        return jnp.where(usable, value, -1).astype(F32)

    tags = jnp.concatenate(
        [
            marked(slot * LANES + permuted(site)),
            marked(slot * LANES + site),
            marked(lower * LANES + permuted(site)),
            marked(lower * LANES + site),
            jnp.where(usable, -weight * (strength_l * rate_l), 0.0),
            jnp.where(usable, weight * strength_l, 0.0),
            jnp.zeros((LANES - 6, LANES), F32),
        ],
        axis=0,
    ).T
    tag_cols[...] = tags
    for c in range(2):
        half = tag_cols[pl.ds(c, TILES, stride=2), :]
        own_cols[c * TILES : (c + 1) * TILES, :] = half
        tag_out[pl.ds(c, TILES, stride=8), :] = half
    tag_tiles = tag_out.reshape(TILES, 8, LANES)
    tag_in_tiles = tag_in.reshape(TILES, 8, LANES)
    up_tiles = up_out.reshape(TILES, 8, LANES)
    up_in_tiles = up_in.reshape(TILES, 8, LANES)
    reply_tiles = reply_out.reshape(TILES, 8, LANES)
    reply_in_tiles = reply_in.reshape(TILES, 8, LANES)

    def exchange(source, target, rows, which, step_tier, allowed):
        other = tier + step_tier

        @pl.when(allowed)
        def _():
            def far(step, carry):
                q = far_first(step)
                pltpu.make_async_remote_copy(
                    source.at[PEERS + q, pl.ds(0, rows)],
                    target.at[PEERS + peer, pl.ds(0, rows)],
                    send_sem.at[which],
                    recv_sem.at[2 * which + 1],
                    device_id=(other, q),
                    device_id_type=MESH,
                ).start()
                return carry

            lax.fori_loop(0, PEERS, far, 0)

        def near(step, carry):
            q = far_first(step)
            pltpu.make_async_remote_copy(
                source.at[q, pl.ds(0, rows)],
                target.at[peer, pl.ds(0, rows)],
                send_sem.at[which],
                recv_sem.at[2 * which],
                device_id=(tier, q),
                device_id_type=MESH,
            ).start()
            return carry

        lax.fori_loop(0, PEERS - 1, near, 0)

    def await_all(target, rows, which, near_sem, far_sem, far_allowed):
        block = target.at[pl.ds(0, PEERS - 1), pl.ds(0, rows)]
        pltpu.make_async_copy(block, block, near_sem).wait()

        @pl.when(far_allowed)
        def _():
            block = target.at[pl.ds(0, PEERS), pl.ds(0, rows)]
            pltpu.make_async_copy(block, block, far_sem).wait()

    def received(target, rows, which, far_allowed):
        await_all(target, rows, which, recv_sem.at[2 * which], recv_sem.at[2 * which + 1], far_allowed)

    def sent(target, rows, which, far_allowed):
        await_all(target, rows, which, send_sem.at[which], send_sem.at[which], far_allowed)

    has_lower = tier > 0
    has_upper = tier < TIERS - 1

    self_row = pl.multiple_of(peer * 8, 8)
    tag_in[pl.ds(self_row, 8), :] = tag_out[pl.ds(self_row, 8), :]

    @pl.when(tier == TIERS - 1)
    def _():
        tag_in[PEERS * 8 :, :] = jnp.full((PEERS * 8, LANES), -1.0, F32)
        up_in[PEERS * 8 :, :] = jnp.zeros((PEERS * 8, LANES), F32)

    @pl.when(tier == 0)
    def _():
        reply_in[PEERS * 8 :, :] = jnp.zeros((PEERS * 8, LANES), F32)

    pl.semaphore_wait(barrier, jnp.where(has_lower, 2 * PEERS - 1, PEERS - 1))

    exchange(tag_tiles, tag_in_tiles, 2, 0, -1, has_lower)

    load.wait()
    lane48 = lax.broadcasted_iota(jnp.int32, (HALF, LANES), 1)
    zero48 = jnp.zeros((HALF, LANES), F32)
    for a in range(SLOTS):
        t0 = raw[pl.ds(a, HALF, stride=24), :]
        t1 = raw[pl.ds(8 + a, HALF, stride=24), :]
        t2 = raw[pl.ds(16 + a, HALF, stride=24), :]
        ok = lane48 < SITES
        even_re = jnp.where(ok, t0, zero48)
        even_im = jnp.where(
            lane48 < 32, pltpu.roll(t0, 32, 1), jnp.where(ok, pltpu.roll(t1, 32, 1), zero48)
        )
        odd_re = jnp.where(
            lane48 < 64, pltpu.roll(t1, 64, 1), jnp.where(ok, pltpu.roll(t2, 64, 1), zero48)
        )
        odd_im = jnp.where(ok, pltpu.roll(t2, 96, 1), zero48)
        gap = jnp.zeros((LANES - SITES, LANES), F32)
        real = jnp.concatenate([even_re, odd_re, gap], axis=0)
        imag = jnp.concatenate([even_im, odd_im, gap], axis=0)
        both = jnp.concatenate([real, imag], axis=1)
        high, low = split_pair(both)
        block = slice(a * LANES, (a + 1) * LANES)
        rows_hi[block, :] = high
        rows_lo[block, :] = low
        turned = jnp.concatenate([real.T, imag.T], axis=1)
        high, low = split_pair(turned)
        cols_hi[block, :] = high
        cols_lo[block, :] = low

    lane1024 = lax.broadcasted_iota(jnp.int32, (LANES, SLOTS * LANES), 1).astype(F32)

    def one_hot(column):
        return jnp.where(
            lane1024 == jnp.broadcast_to(column, (LANES, SLOTS * LANES)), 1.0, 0.0
        ).astype(BF16)

    def gather(row_hot, col_hot):
        rows = mxu(row_hot, rows_hi[...]) + mxu(row_hot, rows_lo[...])
        cols = mxu(col_hot, cols_hi[...]) + mxu(col_hot, cols_lo[...])
        return rows, cols

    def put_tiles(target, rows, cols):
        for c in range(2):
            lanes = slice(c * TILES, (c + 1) * TILES)
            target[pl.ds(4 * c, TILES, stride=8), :] = rows[lanes, :LANES]
            target[pl.ds(4 * c + 1, TILES, stride=8), :] = rows[lanes, LANES:]
            target[pl.ds(4 * c + 2, TILES, stride=8), :] = cols[lanes, :LANES]
            target[pl.ds(4 * c + 3, TILES, stride=8), :] = cols[lanes, LANES:]

    def get_tiles(source):
        def piece(k):
            return jnp.concatenate(
                [source[pl.ds(4 * c + k, TILES, stride=8), :] for c in range(2)], axis=0
            )

        return piece(0), piece(1), piece(2), piece(3)

    own = own_cols[...]
    own_col_hot = one_hot(own[:, 1:2])
    rows, cols = gather(one_hot(own[:, 0:1]), own_col_hot)
    put_tiles(up_out, rows, cols)
    up_in[pl.ds(self_row, 8), :] = up_out[pl.ds(self_row, 8), :]
    exchange(up_tiles, up_in_tiles, 8, 1, -1, has_lower)

    received(tag_in_tiles, 2, 0, has_upper)
    asked = jnp.concatenate([tag_in[pl.ds(c, TILES, stride=8), :] for c in range(2)], axis=0)
    asked_col_hot = one_hot(asked[:, 3:4])
    rows, cols = gather(one_hot(asked[:, 2:3]), asked_col_hot)
    put_tiles(reply_out, rows, cols)
    exchange(reply_tiles, reply_in_tiles, 8, 2, 1, has_upper)
    reply_in[pl.ds(self_row, 8), :] = reply_out[pl.ds(self_row, 8), :]

    diagonal = lax.broadcasted_iota(jnp.int32, (SITES, SITES), 0) == lax.broadcasted_iota(
        jnp.int32, (SITES, SITES), 1
    )
    coupling = coupling_v[...]
    hamilton = (coupling + coupling.T) * 0.5 + jnp.where(
        diagonal, jnp.broadcast_to(base[:SITES, 3:4], (SITES, SITES)), 0.0
    )
    row_id = lax.broadcasted_iota(jnp.int32, (SITES, SITES), 0)
    natural = jnp.where(row_id < HALF, 2 * row_id, 2 * (row_id - HALF) + 1)
    chooser = jnp.where(
        natural == lax.broadcasted_iota(jnp.int32, (SITES, SITES), 1), 1.0, 0.0
    ).astype(BF16)
    h_hi, h_lo = split_pair(hamilton)
    p_hi = mxu(chooser, h_hi).astype(BF16)
    p_lo = mxu(chooser, h_lo).astype(BF16)
    p_hi = mxu(p_hi, chooser.T).astype(BF16)
    p_lo = mxu(p_lo, chooser.T).astype(BF16)
    gap_r = jnp.zeros((SITES, LANES - SITES), BF16)
    left_hi = jnp.concatenate([p_hi, gap_r], axis=1)
    left_lo = jnp.concatenate([p_lo, gap_r], axis=1)
    gap_b = jnp.zeros((LANES - SITES, LANES), BF16)

    def turned_pair(h):
        square = jnp.concatenate([jnp.concatenate([h, gap_r], axis=1), gap_b], axis=0)
        empty = jnp.zeros((LANES, LANES), BF16)
        return jnp.concatenate(
            [
                jnp.concatenate([empty, square], axis=1),
                jnp.concatenate([-square, empty], axis=1),
            ],
            axis=0,
        )

    right_hi = turned_pair(h_hi)
    right_lo = turned_pair(h_lo)

    edge_slot, edge_site, _ = quanta_of(jnp.minimum(lane, SLOTS * DEPTH - 1))
    (edge_rate,) = look_up(edge_site, [rate_col])
    edge_rate = jnp.where((lane < SLOTS * DEPTH) & (edge_site >= 0), edge_rate, 0.0)
    damping = jnp.sum(
        jnp.where(
            sub8 == jnp.broadcast_to(edge_slot, (SLOTS, LANES)),
            jnp.broadcast_to(edge_rate, (SLOTS, LANES)),
            0.0,
        ),
        axis=1,
        keepdims=True,
    )

    for a in range(SLOTS):
        z_hi = rows_hi[a * LANES : (a + 1) * LANES, :]
        z_lo = rows_lo[a * LANES : (a + 1) * LANES, :]
        left = mxu(left_hi, z_hi) + mxu(left_hi, z_lo) + mxu(left_lo, z_hi)
        z_hi = z_hi[:SITES]
        z_lo = z_lo[:SITES]
        right = mxu(z_hi, right_hi) + mxu(z_lo, right_hi) + mxu(z_hi, right_lo)
        z = z_hi.astype(F32) + z_lo.astype(F32)
        total[a * SITES : (a + 1) * SITES, :] = (
            jnp.concatenate([left[:, LANES:], -left[:, :LANES]], axis=1)
            + right
            - damping[a : a + 1, 0:1] * z
        )

    sub768 = lax.broadcasted_iota(jnp.int32, (SLOTS, SITES, LANES), 1) + LANES * (
        lax.broadcasted_iota(jnp.int32, (SLOTS, SITES, LANES), 0)
    )
    sub768 = sub768.astype(F32).reshape(SLOTS * SITES, LANES)

    def scatter_hots(columns, which, col_hot):
        row = columns.T[which : which + 1, :]
        hot = jnp.where(
            sub768 == jnp.broadcast_to(row, (SLOTS * SITES, LANES)), 1.0, 0.0
        ).astype(BF16)
        return jnp.concatenate([hot, hot], axis=1), jnp.concatenate([col_hot, col_hot], axis=0)

    def scatter(row_hots, col_hots, row_data, col_re, col_im):
        high, low = split_pair(row_data)
        by_row = mxu(row_hots, jnp.concatenate([high, low], axis=0))
        turned = jnp.concatenate([col_re.T[:SITES], col_im.T[:SITES]], axis=0)
        high, low = split_pair(turned)
        by_col = mxu(jnp.concatenate([high, low], axis=1), col_hots)
        return by_row, by_col

    def block_of(parts, a):
        by_row, by_col = parts
        lanes = slice(a * LANES, (a + 1) * LANES)
        return by_row[a * SITES : (a + 1) * SITES] + jnp.concatenate(
            [by_col[:SITES, lanes], by_col[SITES:, lanes]], axis=1
        )

    asked_hots = scatter_hots(asked, 2, asked_col_hot)
    own_hots = scatter_hots(own, 0, own_col_hot)
    received(up_in_tiles, 8, 1, has_upper)
    row_re, row_im, col_re, col_im = get_tiles(up_in)
    parts = scatter(*asked_hots, jnp.concatenate([row_im, -row_re], axis=1), -col_im, col_re)
    for a in range(SLOTS):
        total[a * SITES : (a + 1) * SITES, :] += block_of(parts, a)

    received(reply_in_tiles, 8, 2, has_lower)
    row_re, row_im, col_re, col_im = get_tiles(reply_in)
    shared = jnp.broadcast_to(own[:, 4:5], (LANES, LANES))
    turn = jnp.broadcast_to(own[:, 5:6], (LANES, LANES))
    parts = scatter(
        *own_hots,
        jnp.concatenate([shared * row_re + turn * row_im, shared * row_im - turn * row_re], axis=1),
        shared * col_re - turn * col_im,
        shared * col_im + turn * col_re,
    )
    for a in range(SLOTS):
        value = total[a * SITES : (a + 1) * SITES, :] + block_of(parts, a)
        even_re, odd_re = value[:HALF, :LANES], value[HALF:, :LANES]
        even_im, odd_im = value[:HALF, LANES:], value[HALF:, LANES:]
        even_im = pltpu.roll(even_im, 96, 1)
        odd_re = pltpu.roll(odd_re, 64, 1)
        odd_im = pltpu.roll(odd_im, 32, 1)
        result[pl.ds(a, HALF, stride=24), :] = jnp.where(lane48 < SITES, even_re, even_im)
        result[pl.ds(8 + a, HALF, stride=24), :] = jnp.where(lane48 < 64, even_im, odd_re)
        result[pl.ds(16 + a, HALF, stride=24), :] = jnp.where(lane48 < 32, odd_re, odd_im)
    sent(tag_in_tiles, 2, 0, has_lower)
    sent(up_in_tiles, 8, 1, has_lower)
    sent(reply_in_tiles, 8, 2, has_upper)


def on_device(
    section_state,
    coupling,
    site_energy,
    bath_rate,
    bath_strength,
    bath_of_site,
    quanta,
    send_list,
    dest_slot,
):
    slots, width = section_state.shape
    chunks = width // LANES
    tiled = section_state.reshape(slots, chunks, LANES).transpose(1, 0, 2).reshape(-1, LANES)
    operands = (
        tiled,
        coupling,
        site_energy.reshape(1, SITES),
        bath_rate.reshape(1, SITES),
        bath_strength.reshape(1, SITES),
        bath_of_site.reshape(1, SITES),
        quanta.T,
        send_list,
        dest_slot,
    )
    tile_buffer = pltpu.VMEM((TILES * 8, LANES), F32)
    out = pl.pallas_call(
        kernel,
        out_shape=pltpu.VMEM(tiled.shape, F32),
        in_specs=[pl.BlockSpec(memory_space=pltpu.HBM)] * 9,
        out_specs=pl.BlockSpec(memory_space=pltpu.VMEM),
        scratch_shapes=[
            pltpu.VMEM(tiled.shape, F32),
            pltpu.VMEM((SITES, SITES), F32),
            pltpu.VMEM((3, 1, SITES), F32),
            pltpu.VMEM((1, SITES), jnp.int32),
            pltpu.VMEM((DEPTH, SLOTS), jnp.int32),
            pltpu.VMEM((1, LANES), jnp.int32),
            pltpu.VMEM((1, LANES), jnp.int32),
            tile_buffer,
            tile_buffer,
            tile_buffer,
            tile_buffer,
            tile_buffer,
            tile_buffer,
            pltpu.VMEM((LANES, LANES), F32),
            pltpu.VMEM((LANES, LANES), F32),
            pltpu.VMEM((SLOTS * LANES, 2 * LANES), BF16),
            pltpu.VMEM((SLOTS * LANES, 2 * LANES), BF16),
            pltpu.VMEM((SLOTS * LANES, 2 * LANES), BF16),
            pltpu.VMEM((SLOTS * LANES, 2 * LANES), BF16),
            pltpu.VMEM((SLOTS * SITES, 2 * LANES), F32),
            pltpu.SemaphoreType.DMA,
            pltpu.SemaphoreType.DMA((8,)),
            pltpu.SemaphoreType.DMA((3,)),
            pltpu.SemaphoreType.DMA((6,)),
        ],
        compiler_params=pltpu.CompilerParams(
            collective_id=0, has_side_effects=True, vmem_limit_bytes=32 * 1024 * 1024
        ),
    )(*[pltpu.with_memory_space_constraint(value, pltpu.HBM) for value in operands])
    return out.reshape(chunks, slots, LANES).transpose(1, 0, 2).reshape(slots, width)


def solution(mesh):
    return jax.shard_map(
        on_device,
        mesh=mesh,
        in_specs=(
            P(("tier", "aux"), None),
            P(),
            P(),
            P(),
            P(),
            P(),
            P(("tier", "aux"), None),
            P(("tier", "aux"), None),
            P(("tier", "aux"), None),
        ),
        out_specs=P(("tier", "aux"), None),
        check_vma=False,
    )
```

time: 873 us -> 21.7 us (0.02)
  the two profiles are of different devices: /device:TPU:128 before, /device:TPU:97 now
where the time goes in v1:
time: 21.7 us; the launch traced here: 21.6 us
  Pallas kernels  20.7 us (95%)
  local copies, waits for them, and re-layouts  0.82 us (4%)
    pallas_call x1, Pallas kernels, on_device(): pl.pallas_call(kernel, out_shape=pltpu.VMEM(tiled.shape, F32), in_specs=[...  20.7 us
    unnamed x1, local copies, waits for them, and re-layouts  0.82 us

profile of v1, /device:TPU:97, one launch (start us, length us, event | category | flops | bytes accessed | tf_op | source)
XLA Modules:
  0.0 21.6 jit_solution(8691215792843216622)
XLA Ops:
  0.0 20.7 %shard_map.91 = f32[1152,128]{1,0:T(8,128)S(1)} custom-call(f32[1152,128]{1,0:T(8,128)} %bitcast.16, f32[96,96]{1,0:T(8,128)} %coupling_hbm.1, f32[1,96]{1,0:T(1,128)} %bitcast.18, f32[1,96]{1,0:T(1,128)} %bitcast.19, f32[1,96]{1,0:T(1,128)} %bitcast.20, s32[1,96]{1,0:T(1,128)} %bitcast.21, s32[4,8]{1,0:T(4,128)} %bitcast.17, s32[1,128]{1,0:T(1,128)} %send_hbm.1, ...), custom_call_target="tpu_custom_call" | custom-call | tf_op jit(solution)/shard_map/pallas_call | solution.py:504
  20.7 0.8 %copy.11 = f32[8,18432]{1,0:T(8,128)} copy(f32[8,18432]{1,0:T(8,128)S(1)} %bitcast.15) | data formatting | bytes 1179648

commit v2 on v1

--- a/solution.py
+++ b/solution.py
@@ -18,6 +18,21 @@
 TILES = 2 * PEERS
 LANES = 128
 TIERS = 8
+
+
+def routes():
+    found = [
+        (across, dy, dx, dc)
+        for across in range(2)
+        for dy in range(4)
+        for dx in range(4)
+        for dc in range(2)
+        if (across, dy, dx, dc) != (0, 0, 0, 0)
+    ]
+    return sorted(found, key=lambda s: (-(s[0] + min(s[1], 4 - s[1]) + min(s[2], 4 - s[2])), -s[3]))
+
+
+ROUTES = routes()
 
 
 def split_pair(value):
@@ -75,34 +90,34 @@
     my_x = lax.rem(peer, 8) // 2
     my_c = lax.rem(peer, 2)
 
-    def far_first(step):
-        def offset(k):
-            return jnp.where(k == 0, 2, jnp.where(k == 1, 1, jnp.where(k == 2, 3, 0)))
-
-        dy = offset(step // 8)
-        dx = offset(lax.rem(step, 8) // 2)
-        dc = 1 - lax.rem(step, 2)
+    def partner(dy, dx, dc):
         return lax.rem(my_y + dy, 4) * 8 + lax.rem(my_x + dx, 4) * 2 + lax.rem(my_c + dc, 2)
 
     barrier = pltpu.get_barrier_semaphore()
 
-    @pl.when(tier < TIERS - 1)
-    def _():
-        def greet_above(step, carry):
-            pl.semaphore_signal(
-                barrier, inc=1, device_id=(tier + 1, far_first(step)), device_id_type=MESH
-            )
-            return carry
-
-        lax.fori_loop(0, PEERS, greet_above, 0)
-
-    def greet_band(step, carry):
+    def greet(up, dy, dx, dc):
         pl.semaphore_signal(
-            barrier, inc=1, device_id=(tier, far_first(step)), device_id_type=MESH
-        )
-        return carry
-
-    lax.fori_loop(0, PEERS - 1, greet_band, 0)
+            barrier,
+            inc=1,
+            device_id=(tier + up, partner(dy, dx, dc)),
+            device_id_type=MESH,
+        )
+
+    def farthest_first(act, allowed):
+        @pl.when(allowed)
+        def _():
+            for hop in ROUTES:
+                act(*hop)
+
+        @pl.when(jnp.logical_not(allowed))
+        def _():
+            for hop in ROUTES:
+                if not hop[0]:
+                    act(*hop)
+
+    has_lower = tier > 0
+    has_upper = tier < TIERS - 1
+    farthest_first(greet, has_upper)
 
     small = [
         pltpu.make_async_copy(send_hbm, send_v, small_sem.at[0]),
@@ -214,37 +229,18 @@
     reply_in_tiles = reply_in.reshape(TILES, 8, LANES)
 
     def exchange(source, target, rows, which, step_tier, allowed):
-        other = tier + step_tier
-
-        @pl.when(allowed)
-        def _():
-            def far(step, carry):
-                q = far_first(step)
-                pltpu.make_async_remote_copy(
-                    source.at[PEERS + q, pl.ds(0, rows)],
-                    target.at[PEERS + peer, pl.ds(0, rows)],
-                    send_sem.at[which],
-                    recv_sem.at[2 * which + 1],
-                    device_id=(other, q),
-                    device_id_type=MESH,
-                ).start()
-                return carry
-
-            lax.fori_loop(0, PEERS, far, 0)
-
-        def near(step, carry):
-            q = far_first(step)
+        def send(across, dy, dx, dc):
+            q = partner(dy, dx, dc)
             pltpu.make_async_remote_copy(
-                source.at[q, pl.ds(0, rows)],
-                target.at[peer, pl.ds(0, rows)],
+                source.at[PEERS * across + q, pl.ds(0, rows)],
+                target.at[PEERS * across + peer, pl.ds(0, rows)],
                 send_sem.at[which],
-                recv_sem.at[2 * which],
-                device_id=(tier, q),
+                recv_sem.at[2 * which + across],
+                device_id=(tier + step_tier * across, q),
                 device_id_type=MESH,
             ).start()
-            return carry
-
-        lax.fori_loop(0, PEERS - 1, near, 0)
+
+        farthest_first(send, allowed)
 
     def await_all(target, rows, which, near_sem, far_sem, far_allowed):
         block = target.at[pl.ds(0, PEERS - 1), pl.ds(0, rows)]
@@ -260,9 +256,6 @@
 
     def sent(target, rows, which, far_allowed):
         await_all(target, rows, which, send_sem.at[which], send_sem.at[which], far_allowed)
-
-    has_lower = tier > 0
-    has_upper = tier < TIERS - 1
 
     self_row = pl.multiple_of(peer * 8, 8)
     tag_in[pl.ds(self_row, 8), :] = tag_out[pl.ds(self_row, 8), :]

time: 21.7 us -> 20.2 us (0.931)
  the two profiles are of different devices: /device:TPU:97 before, /device:TPU:128 now
where the time goes in v2:
time: 20.2 us; the launch traced here: 20.1 us
  Pallas kernels  19.3 us (96%)
  local copies, waits for them, and re-layouts  0.82 us (4%)
    pallas_call x1, Pallas kernels, on_device(): pl.pallas_call(kernel, out_shape=pltpu.VMEM(tiled.shape, F32), in_specs=[...  19.3 us
    unnamed x1, local copies, waits for them, and re-layouts  0.82 us

profile of v2, /device:TPU:128, one launch (start us, length us, event | category | flops | bytes accessed | tf_op | source)
XLA Modules:
  0.0 20.1 jit_solution(2955296082974281259)
XLA Ops:
  0.0 19.3 %shard_map.91 = f32[1152,128]{1,0:T(8,128)S(1)} custom-call(f32[1152,128]{1,0:T(8,128)} %bitcast.16, f32[96,96]{1,0:T(8,128)} %coupling_hbm.1, f32[1,96]{1,0:T(1,128)} %bitcast.18, f32[1,96]{1,0:T(1,128)} %bitcast.19, f32[1,96]{1,0:T(1,128)} %bitcast.20, s32[1,96]{1,0:T(1,128)} %bitcast.21, s32[4,8]{1,0:T(4,128)} %bitcast.17, s32[1,128]{1,0:T(1,128)} %send_hbm.1, ...), custom_call_target="tpu_custom_call" | custom-call | tf_op jit(solution)/shard_map/pallas_call | solution.py:497
  19.3 0.8 %copy.11 = f32[8,18432]{1,0:T(8,128)} copy(f32[8,18432]{1,0:T(8,128)S(1)} %bitcast.15) | data formatting | bytes 1179648

commit v3 on v2

--- a/solution.py
+++ b/solution.py
@@ -14,6 +14,7 @@
 HALF = 48
 SLOTS = 8
 DEPTH = 4
+PIECES = 3
 PEERS = 32
 TILES = 2 * PEERS
 LANES = 128
@@ -42,10 +43,6 @@
 
 def mxu(left, right):
     return jnp.dot(left, right, preferred_element_type=F32)
-
-
-def permuted(site):
-    return (site >> 1) + HALF * (site & 1)
 
 
 def kernel(
@@ -76,8 +73,9 @@
     own_cols,
     rows_hi,
     rows_lo,
-    cols_hi,
-    cols_lo,
+    natural,
+    table_hi,
+    table_lo,
     total,
     load_sem,
     small_sem,
@@ -204,23 +202,20 @@
     def marked(value):
         return jnp.where(usable, value, -1).astype(F32)
 
+    tag_cols[...] = jnp.broadcast_to(marked(lower * SITES + site), (LANES, LANES)).T
+    for c in range(2):
+        tag_out[pl.ds(c, TILES, stride=8), :] = tag_cols[pl.ds(c, TILES, stride=2), :]
     tags = jnp.concatenate(
         [
-            marked(slot * LANES + permuted(site)),
-            marked(slot * LANES + site),
-            marked(lower * LANES + permuted(site)),
-            marked(lower * LANES + site),
+            marked(slot * SITES + site),
             jnp.where(usable, -weight * (strength_l * rate_l), 0.0),
             jnp.where(usable, weight * strength_l, 0.0),
-            jnp.zeros((LANES - 6, LANES), F32),
+            jnp.zeros((LANES - 3, LANES), F32),
         ],
         axis=0,
     ).T
-    tag_cols[...] = tags
-    for c in range(2):
-        half = tag_cols[pl.ds(c, TILES, stride=2), :]
-        own_cols[c * TILES : (c + 1) * TILES, :] = half
-        tag_out[pl.ds(c, TILES, stride=8), :] = half
+    own_cols[...] = tags
+    own = jnp.concatenate([own_cols[pl.ds(c, TILES, stride=2), :] for c in range(2)], axis=0)
     tag_tiles = tag_out.reshape(TILES, 8, LANES)
     tag_in_tiles = tag_in.reshape(TILES, 8, LANES)
     up_tiles = up_out.reshape(TILES, 8, LANES)
@@ -275,74 +270,93 @@
 
     load.wait()
     lane48 = lax.broadcasted_iota(jnp.int32, (HALF, LANES), 1)
+    lane96 = lax.broadcasted_iota(jnp.int32, (SITES, LANES), 1)
     zero48 = jnp.zeros((HALF, LANES), F32)
+    gap = jnp.zeros((LANES - SITES, LANES), F32)
+    ok = lane48 < SITES
     for a in range(SLOTS):
         t0 = raw[pl.ds(a, HALF, stride=24), :]
         t1 = raw[pl.ds(8 + a, HALF, stride=24), :]
         t2 = raw[pl.ds(16 + a, HALF, stride=24), :]
-        ok = lane48 < SITES
-        even_re = jnp.where(ok, t0, zero48)
+        odd0 = jnp.where(lane48 < 64, pltpu.roll(t1, 64, 1), pltpu.roll(t2, 64, 1))
+        odd1 = pltpu.roll(t2, 64, 1)
+        left_at, right_at = a * SITES, (SLOTS + a) * SITES
+        natural[pl.ds(left_at, HALF, stride=2), :] = t0
+        natural[pl.ds(right_at, HALF, stride=2), :] = t1
+        natural[pl.ds(left_at + 1, HALF, stride=2), :] = odd0
+        natural[pl.ds(right_at + 1, HALF, stride=2), :] = odd1
         even_im = jnp.where(
             lane48 < 32, pltpu.roll(t0, 32, 1), jnp.where(ok, pltpu.roll(t1, 32, 1), zero48)
         )
-        odd_re = jnp.where(
-            lane48 < 64, pltpu.roll(t1, 64, 1), jnp.where(ok, pltpu.roll(t2, 64, 1), zero48)
-        )
         odd_im = jnp.where(ok, pltpu.roll(t2, 96, 1), zero48)
-        gap = jnp.zeros((LANES - SITES, LANES), F32)
-        real = jnp.concatenate([even_re, odd_re, gap], axis=0)
+        real = jnp.concatenate(
+            [jnp.where(ok, t0, zero48), jnp.where(ok, odd0, zero48), gap], axis=0
+        )
         imag = jnp.concatenate([even_im, odd_im, gap], axis=0)
-        both = jnp.concatenate([real, imag], axis=1)
-        high, low = split_pair(both)
+        high, low = split_pair(jnp.concatenate([real, imag], axis=1))
         block = slice(a * LANES, (a + 1) * LANES)
         rows_hi[block, :] = high
         rows_lo[block, :] = low
-        turned = jnp.concatenate([real.T, imag.T], axis=1)
-        high, low = split_pair(turned)
-        cols_hi[block, :] = high
-        cols_lo[block, :] = low
-
-    lane1024 = lax.broadcasted_iota(jnp.int32, (LANES, SLOTS * LANES), 1).astype(F32)
-
-    def one_hot(column):
-        return jnp.where(
-            lane1024 == jnp.broadcast_to(column, (LANES, SLOTS * LANES)), 1.0, 0.0
-        ).astype(BF16)
-
-    def gather(row_hot, col_hot):
-        rows = mxu(row_hot, rows_hi[...]) + mxu(row_hot, rows_lo[...])
-        cols = mxu(col_hot, cols_hi[...]) + mxu(col_hot, cols_lo[...])
-        return rows, cols
-
-    def put_tiles(target, rows, cols):
+        turned_re = pltpu.roll(real.T[:SITES], 64, 1)
+        turned_im = pltpu.roll(imag.T[:SITES], 32, 1)
+        block = slice(a * SITES, (a + 1) * SITES)
+        high, low = split_pair(
+            jnp.concatenate(
+                [
+                    natural[left_at : left_at + SITES, :],
+                    jnp.where(
+                        lane96 < 64, natural[right_at : right_at + SITES, :], turned_re
+                    ),
+                    jnp.where(lane96 < 32, turned_re, turned_im),
+                ],
+                axis=1,
+            )
+        )
+        table_hi[block, :] = high
+        table_lo[block, :] = low
+
+    lane_f = lax.broadcasted_iota(jnp.int32, (LANES, LANES), 1).astype(F32)
+
+    def one_hot(index, chunks):
+        return jnp.concatenate(
+            [
+                jnp.where(lane_f == index - float(LANES * k), 1.0, 0.0).astype(BF16)
+                for k in range(chunks)
+            ],
+            axis=1,
+        )
+
+    def gather(index):
+        hot = one_hot(index, SLOTS * SITES // LANES)
+        return mxu(hot, table_hi[...]) + mxu(hot, table_lo[...])
+
+    def put_tiles(target, packed):
         for c in range(2):
-            lanes = slice(c * TILES, (c + 1) * TILES)
-            target[pl.ds(4 * c, TILES, stride=8), :] = rows[lanes, :LANES]
-            target[pl.ds(4 * c + 1, TILES, stride=8), :] = rows[lanes, LANES:]
-            target[pl.ds(4 * c + 2, TILES, stride=8), :] = cols[lanes, :LANES]
-            target[pl.ds(4 * c + 3, TILES, stride=8), :] = cols[lanes, LANES:]
+            for k in range(PIECES):
+                target[pl.ds(PIECES * c + k, TILES, stride=8), :] = packed[
+                    c * TILES : (c + 1) * TILES, k * LANES : (k + 1) * LANES
+                ]
 
     def get_tiles(source):
         def piece(k):
             return jnp.concatenate(
-                [source[pl.ds(4 * c + k, TILES, stride=8), :] for c in range(2)], axis=0
+                [source[pl.ds(PIECES * c + k, TILES, stride=8), :] for c in range(2)], axis=0
             )
 
-        return piece(0), piece(1), piece(2), piece(3)
-
-    own = own_cols[...]
-    own_col_hot = one_hot(own[:, 1:2])
-    rows, cols = gather(one_hot(own[:, 0:1]), own_col_hot)
-    put_tiles(up_out, rows, cols)
+        first, middle, last = piece(0), piece(1), piece(2)
+        row_im = jnp.where(lane_f < 32.0, pltpu.roll(first, 32, 1), pltpu.roll(middle, 32, 1))
+        col_re = jnp.where(lane_f < 64.0, pltpu.roll(middle, 64, 1), pltpu.roll(last, 64, 1))
+        return first, row_im, col_re, pltpu.roll(last, 96, 1)
+
+    own_index = jnp.broadcast_to(own[:, 0:1], (LANES, LANES))
+    put_tiles(up_out, gather(own_index))
     up_in[pl.ds(self_row, 8), :] = up_out[pl.ds(self_row, 8), :]
-    exchange(up_tiles, up_in_tiles, 8, 1, -1, has_lower)
+    exchange(up_tiles, up_in_tiles, 2 * PIECES, 1, -1, has_lower)
 
     received(tag_in_tiles, 2, 0, has_upper)
     asked = jnp.concatenate([tag_in[pl.ds(c, TILES, stride=8), :] for c in range(2)], axis=0)
-    asked_col_hot = one_hot(asked[:, 3:4])
-    rows, cols = gather(one_hot(asked[:, 2:3]), asked_col_hot)
-    put_tiles(reply_out, rows, cols)
-    exchange(reply_tiles, reply_in_tiles, 8, 2, 1, has_upper)
+    put_tiles(reply_out, gather(asked))
+    exchange(reply_tiles, reply_in_tiles, 2 * PIECES, 2, 1, has_upper)
     reply_in[pl.ds(self_row, 8), :] = reply_out[pl.ds(self_row, 8), :]
 
     diagonal = lax.broadcasted_iota(jnp.int32, (SITES, SITES), 0) == lax.broadcasted_iota(
@@ -353,9 +367,9 @@
         diagonal, jnp.broadcast_to(base[:SITES, 3:4], (SITES, SITES)), 0.0
     )
     row_id = lax.broadcasted_iota(jnp.int32, (SITES, SITES), 0)
-    natural = jnp.where(row_id < HALF, 2 * row_id, 2 * (row_id - HALF) + 1)
+    site_of_row = jnp.where(row_id < HALF, 2 * row_id, 2 * (row_id - HALF) + 1)
     chooser = jnp.where(
-        natural == lax.broadcasted_iota(jnp.int32, (SITES, SITES), 1), 1.0, 0.0
+        site_of_row == lax.broadcasted_iota(jnp.int32, (SITES, SITES), 1), 1.0, 0.0
     ).astype(BF16)
     h_hi, h_lo = split_pair(hamilton)
     p_hi = mxu(chooser, h_hi).astype(BF16)
@@ -408,17 +422,18 @@
             - damping[a : a + 1, 0:1] * z
         )
 
-    sub768 = lax.broadcasted_iota(jnp.int32, (SLOTS, SITES, LANES), 1) + LANES * (
-        lax.broadcasted_iota(jnp.int32, (SLOTS, SITES, LANES), 0)
-    )
-    sub768 = sub768.astype(F32).reshape(SLOTS * SITES, LANES)
-
-    def scatter_hots(columns, which, col_hot):
-        row = columns.T[which : which + 1, :]
-        hot = jnp.where(
-            sub768 == jnp.broadcast_to(row, (SLOTS * SITES, LANES)), 1.0, 0.0
+    sub768 = lax.broadcasted_iota(jnp.int32, (SLOTS * SITES, LANES), 0).astype(F32)
+
+    def scatter_hots(index):
+        slot_f = jnp.floor((index + 0.5) * (1.0 / SITES))
+        site_f = index - float(SITES) * slot_f
+        half = jnp.floor(site_f * 0.5)
+        in_order = float(SITES) * slot_f + half + float(HALF) * (site_f - 2.0 * half)
+        row_hot = jnp.where(
+            sub768 == jnp.broadcast_to(in_order.T[0:1], (SLOTS * SITES, LANES)), 1.0, 0.0
         ).astype(BF16)
-        return jnp.concatenate([hot, hot], axis=1), jnp.concatenate([col_hot, col_hot], axis=0)
+        col_hot = one_hot(float(LANES) * slot_f + site_f, SLOTS)
+        return jnp.concatenate([row_hot, row_hot], axis=1), jnp.concatenate([col_hot, col_hot], axis=0)
 
     def scatter(row_hots, col_hots, row_data, col_re, col_im):
         high, low = split_pair(row_data)
@@ -435,18 +450,18 @@
             [by_col[:SITES, lanes], by_col[SITES:, lanes]], axis=1
         )
 
-    asked_hots = scatter_hots(asked, 2, asked_col_hot)
-    own_hots = scatter_hots(own, 0, own_col_hot)
-    received(up_in_tiles, 8, 1, has_upper)
+    asked_hots = scatter_hots(asked)
+    own_hots = scatter_hots(own_index)
+    received(up_in_tiles, 2 * PIECES, 1, has_upper)
     row_re, row_im, col_re, col_im = get_tiles(up_in)
     parts = scatter(*asked_hots, jnp.concatenate([row_im, -row_re], axis=1), -col_im, col_re)
     for a in range(SLOTS):
         total[a * SITES : (a + 1) * SITES, :] += block_of(parts, a)
 
-    received(reply_in_tiles, 8, 2, has_lower)
+    received(reply_in_tiles, 2 * PIECES, 2, has_lower)
     row_re, row_im, col_re, col_im = get_tiles(reply_in)
-    shared = jnp.broadcast_to(own[:, 4:5], (LANES, LANES))
-    turn = jnp.broadcast_to(own[:, 5:6], (LANES, LANES))
+    shared = jnp.broadcast_to(own[:, 1:2], (LANES, LANES))
+    turn = jnp.broadcast_to(own[:, 2:3], (LANES, LANES))
     parts = scatter(
         *own_hots,
         jnp.concatenate([shared * row_re + turn * row_im, shared * row_im - turn * row_re], axis=1),
@@ -464,8 +479,8 @@
         result[pl.ds(8 + a, HALF, stride=24), :] = jnp.where(lane48 < 64, even_im, odd_re)
         result[pl.ds(16 + a, HALF, stride=24), :] = jnp.where(lane48 < 32, odd_re, odd_im)
     sent(tag_in_tiles, 2, 0, has_lower)
-    sent(up_in_tiles, 8, 1, has_lower)
-    sent(reply_in_tiles, 8, 2, has_upper)
+    sent(up_in_tiles, 2 * PIECES, 1, has_lower)
+    sent(reply_in_tiles, 2 * PIECES, 2, has_upper)
 
 
 def on_device(
@@ -517,8 +532,9 @@
             pltpu.VMEM((LANES, LANES), F32),
             pltpu.VMEM((SLOTS * LANES, 2 * LANES), BF16),
             pltpu.VMEM((SLOTS * LANES, 2 * LANES), BF16),
-            pltpu.VMEM((SLOTS * LANES, 2 * LANES), BF16),
-            pltpu.VMEM((SLOTS * LANES, 2 * LANES), BF16),
+            pltpu.VMEM((2 * SLOTS * SITES, LANES), F32),
+            pltpu.VMEM((SLOTS * SITES, PIECES * LANES), BF16),
+            pltpu.VMEM((SLOTS * SITES, PIECES * LANES), BF16),
             pltpu.VMEM((SLOTS * SITES, 2 * LANES), F32),
             pltpu.SemaphoreType.DMA,
             pltpu.SemaphoreType.DMA((8,)),

time: 20.2 us -> 19.7 us (0.975)
  Pallas kernels: 19.3 us -> 18.7 us
    pallas_call x1, Pallas kernels: 19.3 us -> 18.7 us  [on_device(): pl.pallas_call(kernel, out_shape=pltpu.VMEM(tiled.shape, F32), in_specs=[...]
where the time goes in v3:
time: 19.7 us; the launch traced here: 19.5 us
  Pallas kernels  18.7 us (95%)
  local copies, waits for them, and re-layouts  0.82 us (4%)
    pallas_call x1, Pallas kernels, on_device(): pl.pallas_call(kernel, out_shape=pltpu.VMEM(tiled.shape, F32), in_specs=[...  18.7 us
    unnamed x1, local copies, waits for them, and re-layouts  0.82 us

profile of v3, /device:TPU:128, one launch (start us, length us, event | category | flops | bytes accessed | tf_op | source)
XLA Modules:
  0.0 19.5 jit_solution(2684047291351407876)
XLA Ops:
  0.0 18.7 %shard_map.91 = f32[1152,128]{1,0:T(8,128)S(1)} custom-call(f32[1152,128]{1,0:T(8,128)} %bitcast.16, f32[96,96]{1,0:T(8,128)} %coupling_hbm.1, f32[1,96]{1,0:T(1,128)} %bitcast.18, f32[1,96]{1,0:T(1,128)} %bitcast.19, f32[1,96]{1,0:T(1,128)} %bitcast.20, s32[1,96]{1,0:T(1,128)} %bitcast.21, s32[4,8]{1,0:T(4,128)} %bitcast.17, s32[1,128]{1,0:T(1,128)} %send_hbm.1, ...), custom_call_target="tpu_custom_call" | custom-call | tf_op jit(solution)/shard_map/pallas_call | solution.py:512
  18.7 0.8 %copy.11 = f32[8,18432]{1,0:T(8,128)} copy(f32[8,18432]{1,0:T(8,128)S(1)} %bitcast.15) | data formatting | bytes 1179648

commit v4 on v3

--- a/solution.py
+++ b/solution.py
@@ -88,8 +88,12 @@
     my_x = lax.rem(peer, 8) // 2
     my_c = lax.rem(peer, 2)
 
+    at_y = [lax.rem(my_y + d, 4) * 8 for d in range(4)]
+    at_x = [lax.rem(my_x + d, 4) * 2 for d in range(4)]
+    at_c = [my_c, 1 - my_c]
+
     def partner(dy, dx, dc):
-        return lax.rem(my_y + dy, 4) * 8 + lax.rem(my_x + dx, 4) * 2 + lax.rem(my_c + dc, 2)
+        return at_y[dy % 4] + at_x[dx % 4] + at_c[dc]
 
     barrier = pltpu.get_barrier_semaphore()
 
@@ -101,11 +105,21 @@
             device_id_type=MESH,
         )
 
-    def farthest_first(act, allowed):
+    def farthest_first(act, allowed, chosen=(0, 1)):
+        if chosen == (0,):
+            for hop in ROUTES:
+                if not hop[0]:
+                    act(*hop)
+            return
+
         @pl.when(allowed)
         def _():
             for hop in ROUTES:
-                act(*hop)
+                if hop[0] in chosen:
+                    act(*hop)
+
+        if 0 not in chosen:
+            return
 
         @pl.when(jnp.logical_not(allowed))
         def _():
@@ -203,8 +217,10 @@
         return jnp.where(usable, value, -1).astype(F32)
 
     tag_cols[...] = jnp.broadcast_to(marked(lower * SITES + site), (LANES, LANES)).T
-    for c in range(2):
-        tag_out[pl.ds(c, TILES, stride=8), :] = tag_cols[pl.ds(c, TILES, stride=2), :]
+    left_half = lax.broadcasted_iota(jnp.int32, (TILES, LANES), 1) < TILES
+    tag_out[pl.ds(0, TILES, stride=8), :] = jnp.where(
+        left_half, tag_cols[pl.ds(0, TILES, stride=2), :], tag_cols[pl.ds(1, TILES, stride=2), :]
+    )
     tags = jnp.concatenate(
         [
             marked(slot * SITES + site),
@@ -215,7 +231,12 @@
         axis=0,
     ).T
     own_cols[...] = tags
-    own = jnp.concatenate([own_cols[pl.ds(c, TILES, stride=2), :] for c in range(2)], axis=0)
+    own = [
+        jnp.concatenate(
+            [own_cols[pl.ds(TILES * g + c, PEERS, stride=2), :] for c in range(2)], axis=0
+        )
+        for g in range(2)
+    ]
     tag_tiles = tag_out.reshape(TILES, 8, LANES)
     tag_in_tiles = tag_in.reshape(TILES, 8, LANES)
     up_tiles = up_out.reshape(TILES, 8, LANES)
@@ -223,7 +244,7 @@
     reply_tiles = reply_out.reshape(TILES, 8, LANES)
     reply_in_tiles = reply_in.reshape(TILES, 8, LANES)
 
-    def exchange(source, target, rows, which, step_tier, allowed):
+    def exchange(source, target, rows, which, step_tier, allowed, chosen=(0, 1)):
         def send(across, dy, dx, dc):
             q = partner(dy, dx, dc)
             pltpu.make_async_remote_copy(
@@ -235,22 +256,27 @@
                 device_id_type=MESH,
             ).start()
 
-        farthest_first(send, allowed)
-
-    def await_all(target, rows, which, near_sem, far_sem, far_allowed):
+        farthest_first(send, allowed, chosen)
+
+    def await_near(target, rows, semaphore):
         block = target.at[pl.ds(0, PEERS - 1), pl.ds(0, rows)]
-        pltpu.make_async_copy(block, block, near_sem).wait()
-
-        @pl.when(far_allowed)
+        pltpu.make_async_copy(block, block, semaphore).wait()
+
+    def await_far(target, rows, semaphore, allowed):
+        @pl.when(allowed)
         def _():
             block = target.at[pl.ds(0, PEERS), pl.ds(0, rows)]
-            pltpu.make_async_copy(block, block, far_sem).wait()
-
-    def received(target, rows, which, far_allowed):
-        await_all(target, rows, which, recv_sem.at[2 * which], recv_sem.at[2 * which + 1], far_allowed)
-
-    def sent(target, rows, which, far_allowed):
-        await_all(target, rows, which, send_sem.at[which], send_sem.at[which], far_allowed)
+            pltpu.make_async_copy(block, block, semaphore).wait()
+
+    def received_near(target, rows, which):
+        await_near(target, rows, recv_sem.at[2 * which])
+
+    def received_far(target, rows, which, allowed):
+        await_far(target, rows, recv_sem.at[2 * which + 1], allowed)
+
+    def sent(target, rows, which, allowed):
+        await_near(target, rows, send_sem.at[which])
+        await_far(target, rows, send_sem.at[which], allowed)
 
     self_row = pl.multiple_of(peer * 8, 8)
     tag_in[pl.ds(self_row, 8), :] = tag_out[pl.ds(self_row, 8), :]
@@ -266,7 +292,7 @@
 
     pl.semaphore_wait(barrier, jnp.where(has_lower, 2 * PEERS - 1, PEERS - 1))
 
-    exchange(tag_tiles, tag_in_tiles, 2, 0, -1, has_lower)
+    exchange(tag_tiles, tag_in_tiles, 1, 0, -1, has_lower)
 
     load.wait()
     lane48 = lax.broadcasted_iota(jnp.int32, (HALF, LANES), 1)
@@ -320,7 +346,7 @@
     def one_hot(index, chunks):
         return jnp.concatenate(
             [
-                jnp.where(lane_f == index - float(LANES * k), 1.0, 0.0).astype(BF16)
+                jnp.where(lane_f[: index.shape[0]] == index - float(LANES * k), 1.0, 0.0).astype(BF16)
                 for k in range(chunks)
             ],
             axis=1,
@@ -330,33 +356,55 @@
         hot = one_hot(index, SLOTS * SITES // LANES)
         return mxu(hot, table_hi[...]) + mxu(hot, table_lo[...])
 
-    def put_tiles(target, packed):
+    def put_tiles(target, g, packed):
         for c in range(2):
             for k in range(PIECES):
-                target[pl.ds(PIECES * c + k, TILES, stride=8), :] = packed[
-                    c * TILES : (c + 1) * TILES, k * LANES : (k + 1) * LANES
+                target[pl.ds(PEERS * 8 * g + PIECES * c + k, PEERS, stride=8), :] = packed[
+                    c * PEERS : (c + 1) * PEERS, k * LANES : (k + 1) * LANES
                 ]
 
-    def get_tiles(source):
+    lane_h = lane_f[: 2 * PEERS]
+
+    def get_tiles(source, g):
         def piece(k):
             return jnp.concatenate(
-                [source[pl.ds(PIECES * c + k, TILES, stride=8), :] for c in range(2)], axis=0
+                [
+                    source[pl.ds(PEERS * 8 * g + PIECES * c + k, PEERS, stride=8), :]
+                    for c in range(2)
+                ],
+                axis=0,
             )
 
         first, middle, last = piece(0), piece(1), piece(2)
-        row_im = jnp.where(lane_f < 32.0, pltpu.roll(first, 32, 1), pltpu.roll(middle, 32, 1))
-        col_re = jnp.where(lane_f < 64.0, pltpu.roll(middle, 64, 1), pltpu.roll(last, 64, 1))
+        row_im = jnp.where(lane_h < 32.0, pltpu.roll(first, 32, 1), pltpu.roll(middle, 32, 1))
+        col_re = jnp.where(lane_h < 64.0, pltpu.roll(middle, 64, 1), pltpu.roll(last, 64, 1))
         return first, row_im, col_re, pltpu.roll(last, 96, 1)
 
-    own_index = jnp.broadcast_to(own[:, 0:1], (LANES, LANES))
-    put_tiles(up_out, gather(own_index))
+    own_index = [jnp.broadcast_to(own[g][:, 0:1], (TILES, LANES)) for g in range(2)]
+    packed = gather(jnp.concatenate(own_index, axis=0))
+    for g in range(2):
+        put_tiles(up_out, g, packed[g * TILES : (g + 1) * TILES])
     up_in[pl.ds(self_row, 8), :] = up_out[pl.ds(self_row, 8), :]
     exchange(up_tiles, up_in_tiles, 2 * PIECES, 1, -1, has_lower)
 
-    received(tag_in_tiles, 2, 0, has_upper)
-    asked = jnp.concatenate([tag_in[pl.ds(c, TILES, stride=8), :] for c in range(2)], axis=0)
-    put_tiles(reply_out, gather(asked))
-    exchange(reply_tiles, reply_in_tiles, 2 * PIECES, 2, 1, has_upper)
+    asked = []
+    for g in range(2):
+        if g == 0:
+            received_near(tag_in_tiles, 1, 0)
+        else:
+            received_far(tag_in_tiles, 1, 0, has_upper)
+        both = tag_in[pl.ds(PEERS * 8 * g, PEERS, stride=8), :]
+        swapped = pltpu.roll(both, TILES, 1)
+        index = jnp.concatenate(
+            [
+                jnp.where(left_half[:PEERS], both, swapped),
+                jnp.where(left_half[:PEERS], swapped, both),
+            ],
+            axis=0,
+        )
+        asked.append(index)
+        put_tiles(reply_out, g, gather(index))
+        exchange(reply_tiles, reply_in_tiles, 2 * PIECES, 2, 1, has_upper if g else True, (g,))
     reply_in[pl.ds(self_row, 8), :] = reply_out[pl.ds(self_row, 8), :]
 
     diagonal = lax.broadcasted_iota(jnp.int32, (SITES, SITES), 0) == lax.broadcasted_iota(
@@ -433,14 +481,17 @@
             sub768 == jnp.broadcast_to(in_order.T[0:1], (SLOTS * SITES, LANES)), 1.0, 0.0
         ).astype(BF16)
         col_hot = one_hot(float(LANES) * slot_f + site_f, SLOTS)
-        return jnp.concatenate([row_hot, row_hot], axis=1), jnp.concatenate([col_hot, col_hot], axis=0)
+        return row_hot, col_hot
 
     def scatter(row_hots, col_hots, row_data, col_re, col_im):
         high, low = split_pair(row_data)
         by_row = mxu(row_hots, jnp.concatenate([high, low], axis=0))
-        turned = jnp.concatenate([col_re.T[:SITES], col_im.T[:SITES]], axis=0)
-        high, low = split_pair(turned)
-        by_col = mxu(jnp.concatenate([high, low], axis=1), col_hots)
+        turned = []
+        for column in (col_re, col_im):
+            high, low = split_pair(column)
+            stacked = jnp.concatenate([high.astype(F32), low.astype(F32)], axis=0)
+            turned.append(stacked.T[:SITES].astype(BF16))
+        by_col = mxu(jnp.concatenate(turned, axis=0), col_hots)
         return by_row, by_col
 
     def block_of(parts, a):
@@ -450,24 +501,40 @@
             [by_col[:SITES, lanes], by_col[SITES:, lanes]], axis=1
         )
 
-    asked_hots = scatter_hots(asked)
-    own_hots = scatter_hots(own_index)
-    received(up_in_tiles, 2 * PIECES, 1, has_upper)
-    row_re, row_im, col_re, col_im = get_tiles(up_in)
-    parts = scatter(*asked_hots, jnp.concatenate([row_im, -row_re], axis=1), -col_im, col_re)
-    for a in range(SLOTS):
-        total[a * SITES : (a + 1) * SITES, :] += block_of(parts, a)
-
-    received(reply_in_tiles, 2 * PIECES, 2, has_lower)
-    row_re, row_im, col_re, col_im = get_tiles(reply_in)
-    shared = jnp.broadcast_to(own[:, 1:2], (LANES, LANES))
-    turn = jnp.broadcast_to(own[:, 2:3], (LANES, LANES))
-    parts = scatter(
-        *own_hots,
-        jnp.concatenate([shared * row_re + turn * row_im, shared * row_im - turn * row_re], axis=1),
-        shared * col_re - turn * col_im,
-        shared * col_im + turn * col_re,
-    )
+    def twice(index):
+        return jnp.concatenate([index, index], axis=0)
+
+    for g in range(2):
+        hots = scatter_hots(twice(asked[g]))
+        if g == 0:
+            received_near(up_in_tiles, 2 * PIECES, 1)
+        else:
+            received_far(up_in_tiles, 2 * PIECES, 1, has_upper)
+        row_re, row_im, col_re, col_im = get_tiles(up_in, g)
+        parts = scatter(*hots, jnp.concatenate([row_im, -row_re], axis=1), -col_im, col_re)
+        for a in range(SLOTS):
+            total[a * SITES : (a + 1) * SITES, :] += block_of(parts, a)
+
+    own_hots = [scatter_hots(twice(own_index[g])) for g in range(2)]
+    for g in range(2):
+        if g == 0:
+            received_near(reply_in_tiles, 2 * PIECES, 2)
+        else:
+            received_far(reply_in_tiles, 2 * PIECES, 2, has_lower)
+        row_re, row_im, col_re, col_im = get_tiles(reply_in, g)
+        shared = jnp.broadcast_to(own[g][:, 1:2], (TILES, LANES))
+        turn = jnp.broadcast_to(own[g][:, 2:3], (TILES, LANES))
+        parts = scatter(
+            *own_hots[g],
+            jnp.concatenate(
+                [shared * row_re + turn * row_im, shared * row_im - turn * row_re], axis=1
+            ),
+            shared * col_re - turn * col_im,
+            shared * col_im + turn * col_re,
+        )
+        if g == 0:
+            for a in range(SLOTS):
+                total[a * SITES : (a + 1) * SITES, :] += block_of(parts, a)
     for a in range(SLOTS):
         value = total[a * SITES : (a + 1) * SITES, :] + block_of(parts, a)
         even_re, odd_re = value[:HALF, :LANES], value[HALF:, :LANES]
@@ -478,7 +545,7 @@
         result[pl.ds(a, HALF, stride=24), :] = jnp.where(lane48 < SITES, even_re, even_im)
         result[pl.ds(8 + a, HALF, stride=24), :] = jnp.where(lane48 < 64, even_im, odd_re)
         result[pl.ds(16 + a, HALF, stride=24), :] = jnp.where(lane48 < 32, odd_re, odd_im)
-    sent(tag_in_tiles, 2, 0, has_lower)
+    sent(tag_in_tiles, 1, 0, has_lower)
     sent(up_in_tiles, 2 * PIECES, 1, has_lower)
     sent(reply_in_tiles, 2 * PIECES, 2, has_upper)
 

time: 19.7 us -> 19.3 us (0.980)
  Pallas kernels: 18.7 us -> 18.4 us
    pallas_call x1, Pallas kernels: 18.7 us -> 18.4 us  [on_device(): pl.pallas_call(kernel, out_shape=pltpu.VMEM(tiled.shape, F32), in_specs=[...]
where the time goes in v4:
time: 19.3 us; the launch traced here: 19.2 us
  Pallas kernels  18.4 us (95%)
  local copies, waits for them, and re-layouts  0.82 us (4%)
    pallas_call x1, Pallas kernels, on_device(): pl.pallas_call(kernel, out_shape=pltpu.VMEM(tiled.shape, F32), in_specs=[...  18.4 us
    unnamed x1, local copies, waits for them, and re-layouts  0.82 us

profile of v4, /device:TPU:128, one launch (start us, length us, event | category | flops | bytes accessed | tf_op | source)
XLA Modules:
  0.0 19.2 jit_solution(18034714308600612626)
XLA Ops:
  0.0 18.4 %shard_map.91 = f32[1152,128]{1,0:T(8,128)S(1)} custom-call(f32[1152,128]{1,0:T(8,128)} %bitcast.16, f32[96,96]{1,0:T(8,128)} %coupling_hbm.1, f32[1,96]{1,0:T(1,128)} %bitcast.18, f32[1,96]{1,0:T(1,128)} %bitcast.19, f32[1,96]{1,0:T(1,128)} %bitcast.20, s32[1,96]{1,0:T(1,128)} %bitcast.21, s32[4,8]{1,0:T(4,128)} %bitcast.17, s32[1,128]{1,0:T(1,128)} %send_hbm.1, ...), custom_call_target="tpu_custom_call" | custom-call | tf_op jit(solution)/shard_map/pallas_call | solution.py:579
  18.4 0.8 %copy.11 = f32[8,18432]{1,0:T(8,128)} copy(f32[8,18432]{1,0:T(8,128)S(1)} %bitcast.15) | data formatting | bytes 1179648

commit v5 on v4

--- a/solution.py
+++ b/solution.py
@@ -74,8 +74,7 @@
     rows_hi,
     rows_lo,
     natural,
-    table_hi,
-    table_lo,
+    table,
     total,
     load_sem,
     small_sem,
@@ -338,8 +337,7 @@
                 axis=1,
             )
         )
-        table_hi[block, :] = high
-        table_lo[block, :] = low
+        table[block, :] = jnp.concatenate([high, low], axis=1)
 
     lane_f = lax.broadcasted_iota(jnp.int32, (LANES, LANES), 1).astype(F32)
 
@@ -354,7 +352,8 @@
 
     def gather(index):
         hot = one_hot(index, SLOTS * SITES // LANES)
-        return mxu(hot, table_hi[...]) + mxu(hot, table_lo[...])
+        found = mxu(hot, table[...])
+        return found[:, : PIECES * LANES] + found[:, PIECES * LANES :]
 
     def put_tiles(target, g, packed):
         for c in range(2):
@@ -600,8 +599,7 @@
             pltpu.VMEM((SLOTS * LANES, 2 * LANES), BF16),
             pltpu.VMEM((SLOTS * LANES, 2 * LANES), BF16),
             pltpu.VMEM((2 * SLOTS * SITES, LANES), F32),
-            pltpu.VMEM((SLOTS * SITES, PIECES * LANES), BF16),
-            pltpu.VMEM((SLOTS * SITES, PIECES * LANES), BF16),
+            pltpu.VMEM((SLOTS * SITES, 2 * PIECES * LANES), BF16),
             pltpu.VMEM((SLOTS * SITES, 2 * LANES), F32),
             pltpu.SemaphoreType.DMA,
             pltpu.SemaphoreType.DMA((8,)),

time: 19.3 us -> 19.3 us (level)
  no operation moved by 1% of the time
where the time goes in v5:
time: 19.3 us; the launch traced here: 19.2 us
  Pallas kernels  18.4 us (95%)
  local copies, waits for them, and re-layouts  0.82 us (4%)
    pallas_call x1, Pallas kernels, on_device(): pl.pallas_call(kernel, out_shape=pltpu.VMEM(tiled.shape, F32), in_specs=[...  18.4 us
    unnamed x1, local copies, waits for them, and re-layouts  0.82 us

profile of v5, /device:TPU:128, one launch (start us, length us, event | category | flops | bytes accessed | tf_op | source)
XLA Modules:
  0.0 19.2 jit_solution(7875380059422121282)
XLA Ops:
  0.0 18.4 %shard_map.91 = f32[1152,128]{1,0:T(8,128)S(1)} custom-call(f32[1152,128]{1,0:T(8,128)} %bitcast.16, f32[96,96]{1,0:T(8,128)} %coupling_hbm.1, f32[1,96]{1,0:T(1,128)} %bitcast.18, f32[1,96]{1,0:T(1,128)} %bitcast.19, f32[1,96]{1,0:T(1,128)} %bitcast.20, s32[1,96]{1,0:T(1,128)} %bitcast.21, s32[4,8]{1,0:T(4,128)} %bitcast.17, s32[1,128]{1,0:T(1,128)} %send_hbm.1, ...), custom_call_target="tpu_custom_call" | custom-call | tf_op jit(solution)/shard_map/pallas_call | solution.py:578
  18.4 0.8 %copy.11 = f32[8,18432]{1,0:T(8,128)} copy(f32[8,18432]{1,0:T(8,128)S(1)} %bitcast.15) | data formatting | bytes 1179648

commit v6 on v5

--- a/solution.py
+++ b/solution.py
@@ -386,24 +386,41 @@
     up_in[pl.ds(self_row, 8), :] = up_out[pl.ds(self_row, 8), :]
     exchange(up_tiles, up_in_tiles, 2 * PIECES, 1, -1, has_lower)
 
-    asked = []
-    for g in range(2):
-        if g == 0:
-            received_near(tag_in_tiles, 1, 0)
-        else:
-            received_far(tag_in_tiles, 1, 0, has_upper)
+    def asked_of(g):
         both = tag_in[pl.ds(PEERS * 8 * g, PEERS, stride=8), :]
         swapped = pltpu.roll(both, TILES, 1)
-        index = jnp.concatenate(
+        return jnp.concatenate(
             [
                 jnp.where(left_half[:PEERS], both, swapped),
                 jnp.where(left_half[:PEERS], swapped, both),
             ],
             axis=0,
         )
-        asked.append(index)
-        put_tiles(reply_out, g, gather(index))
-        exchange(reply_tiles, reply_in_tiles, 2 * PIECES, 2, 1, has_upper if g else True, (g,))
+
+    def answer(g):
+        put_tiles(reply_out, g, gather(asked_of(g)))
+        for across, dy, dx, dc in ROUTES:
+            if across == g:
+                q = partner(dy, dx, dc)
+                pltpu.make_async_remote_copy(
+                    reply_tiles.at[PEERS * g + q, pl.ds(0, 2 * PIECES)],
+                    reply_in_tiles.at[PEERS * g + peer, pl.ds(0, 2 * PIECES)],
+                    send_sem.at[2],
+                    recv_sem.at[4 + g],
+                    device_id=(tier + g, q),
+                    device_id_type=MESH,
+                ).start()
+
+    received_near(tag_in_tiles, 1, 0)
+    answer(0)
+
+    @pl.when(has_upper)
+    def _():
+        block = tag_in_tiles.at[pl.ds(0, PEERS), pl.ds(0, 1)]
+        pltpu.make_async_copy(block, block, recv_sem.at[1]).wait()
+        answer(1)
+
+    asked = [asked_of(g) for g in range(2)]
     reply_in[pl.ds(self_row, 8), :] = reply_out[pl.ds(self_row, 8), :]
 
     diagonal = lax.broadcasted_iota(jnp.int32, (SITES, SITES), 0) == lax.broadcasted_iota(

time: 19.3 us -> 19.3 us (level)
  no operation moved by 1% of the time
where the time goes in v6:
time: 19.3 us; the launch traced here: 19.2 us
  Pallas kernels  18.3 us (95%)
  local copies, waits for them, and re-layouts  0.82 us (4%)
    pallas_call x1, Pallas kernels, on_device(): pl.pallas_call(kernel, out_shape=pltpu.VMEM(tiled.shape, F32), in_specs=[...  18.3 us
    unnamed x1, local copies, waits for them, and re-layouts  0.82 us

profile of v6, /device:TPU:128, one launch (start us, length us, event | category | flops | bytes accessed | tf_op | source)
XLA Modules:
  0.0 19.2 jit_solution(18280668472898382877)
XLA Ops:
  0.0 18.3 %shard_map.91 = f32[1152,128]{1,0:T(8,128)S(1)} custom-call(f32[1152,128]{1,0:T(8,128)} %bitcast.16, f32[96,96]{1,0:T(8,128)} %coupling_hbm.1, f32[1,96]{1,0:T(1,128)} %bitcast.18, f32[1,96]{1,0:T(1,128)} %bitcast.19, f32[1,96]{1,0:T(1,128)} %bitcast.20, s32[1,96]{1,0:T(1,128)} %bitcast.21, s32[4,8]{1,0:T(4,128)} %bitcast.17, s32[1,128]{1,0:T(1,128)} %send_hbm.1, ...), custom_call_target="tpu_custom_call" | custom-call | tf_op jit(solution)/shard_map/pallas_call | solution.py:595
  18.4 0.8 %copy.11 = f32[8,18432]{1,0:T(8,128)} copy(f32[8,18432]{1,0:T(8,128)S(1)} %bitcast.15) | data formatting | bytes 1179648
